TPU v7x, 128 devices: a whole 4x4x4 slice. The times are simulated.
128 devices in a mesh: batch: 16 (over y, z), head: 8 (over x, core).
Axes of the slice: x: 4, y: 4, z: 4, core: 2. Of those that a mesh axis runs over, the one named last changes fastest.
Arguments:
- hidden_in: bfloat16 [1024, 3, 2048], P(('batch', 'head')), may hold values from -6 to 6
- states: float32 [1024, 16, 128, 128], P('batch', 'head'), may hold values from -0.8 to 0.8
- norm_in: float32 [2048], replicated, may hold values from 0.1 to 1.9
- w_qk: bfloat16 [2048, 8, 2, 128], P(None, 'head'), may hold values from -0.125 to 0.125
- w_vz: bfloat16 [2048, 16, 2, 128], P(None, 'head'), may hold values from -0.125 to 0.125
- w_ba: bfloat16 [2048, 2, 16], P(None, None, 'head'), may hold values from -0.125 to 0.125
- a_log: float32 [16], P('head'), may hold values from -4 to 1.5
- dt_bias: float32 [16], P('head'), may hold values from -2 to 1
- norm_gate: float32 [128], replicated, may hold values from 0.1 to 1.9
- w_out: bfloat16 [16, 128, 2048], P('head'), may hold values from -0.125 to 0.125
- norm_post: float32 [2048], replicated, may hold values from 0.1 to 1.9
- shared_in: bfloat16 [2048, 2, 512], P('head'), may hold values from -0.125 to 0.125
- shared_gate: bfloat16 [2048], P('head'), may hold values from -0.125 to 0.125
- shared_out: bfloat16 [512, 2048], P(None, 'head'), may hold values from -0.25 to 0.25
- expert_in: bfloat16 [256, 2048, 2, 512], P(('batch', 'head')), may hold values from -0.125 to 0.125
- expert_out: bfloat16 [256, 512, 2048], P(('batch', 'head')), may hold values from -0.25 to 0.25
- routes: int32 [1024, 3, 10], P(('batch', 'head')), may hold values from 0 to 255, all different within a row; in each aligned block of 24 rows (0 to 23, 24 to 47, ..., all dimensions but the last counted through in order) at most 2 rows name the same one
- route_weight: float32 [1024, 3, 10], P(('batch', 'head')), may hold values from 0.02 to 0.25
Outputs:
- layer_out: bfloat16 [1024, 3, 2048], P('batch', None, 'head')
Inputs may be any that keep to these rules, and one draw needn't show every extreme that they name: `routes`: among the 240 choices of one device's tokens, no expert is named more than 2 times, a bound that some block reaches; a token's 10 experts differ.
All inputs are finite; a program needn't handle non-finite values.
Results may differ from a plain program's by a relative error of at most 0.009.
Values may be sent and summed in bfloat16 or wider, within the bound.
A program may use at most 128 MiB of HBM per device.

v0:
```python
import functools

import jax
import jax.numpy as jnp
from jax import lax
from jax.experimental import pallas as pl
from jax.experimental.pallas import tpu as pltpu
from jax.sharding import PartitionSpec as P

EPS = 1e-06
MESH = pl.DeviceIdType.MESH
HEADS = 8
BATCH = 16
DEVS = HEADS * BATCH
F32 = jnp.float32
BF16 = jnp.bfloat16
VMEM = pl.BlockSpec(memory_space=pltpu.VMEM)


def rms_scale(values, gain):
    return values * lax.rsqrt(jnp.mean(values * values, axis=-1, keepdims=True) + EPS) * gain


def silu(v):
    return v * jax.nn.sigmoid(v)


def spot(p):
    return (p // HEADS, p % HEADS)


def gather_kernel(own_ref, all_ref, send_sem, recv_sem, local_sem):
    b = lax.axis_index("batch")
    h = lax.axis_index("head")
    x, c = h // 2, h % 2
    sib = x * 2 + 1 - c
    chips = [(x + d) % 4 for d in (1, 3, 2)]
    barrier = pltpu.get_barrier_semaphore()
    for to in [sib] + [v * 2 + c for v in chips]:
        pl.semaphore_signal(barrier, inc=1, device_id=(b, to), device_id_type=MESH)
    pl.semaphore_wait(barrier, 4)
    mine = pltpu.make_async_copy(own_ref, all_ref.at[:, h], local_sem)
    mine.start()
    sent = []

    def send(src, slot, to):
        copy = pltpu.make_async_remote_copy(
            src_ref=src,
            dst_ref=all_ref.at[:, slot],
            send_sem=send_sem.at[len(sent)],
            recv_sem=recv_sem.at[slot],
            device_id=(b, to),
            device_id_type=MESH,
        )
        copy.start()
        sent.append(copy)

    def arrived(slot):
        pltpu.make_async_copy(own_ref, all_ref.at[:, slot], recv_sem.at[slot]).wait()

    for v in chips:
        send(own_ref, h, v * 2 + c)
    send(own_ref, h, sib)
    for d in (3, 1, 2):
        slot = ((x + d) % 4) * 2 + c
        arrived(slot)
        send(all_ref.at[:, slot], slot, sib)
    for d in (0, 3, 1, 2):
        arrived(((x + d) % 4) * 2 + 1 - c)
    mine.wait()
    for copy in sent:
        copy.wait_send()


def gather_head(own):
    return pl.pallas_call(
        gather_kernel,
        name="gather_input",
        out_shape=jax.ShapeDtypeStruct((3, HEADS) + own.shape[1:], own.dtype),
        in_specs=[VMEM],
        out_specs=VMEM,
        scratch_shapes=[
            pltpu.SemaphoreType.DMA((7,)),
            pltpu.SemaphoreType.DMA((HEADS,)),
            pltpu.SemaphoreType.DMA(()),
        ],
        compiler_params=pltpu.CompilerParams(collective_id=0, has_side_effects=True),
    )(own)


def delta_kernel(qk_ref, vz_ref, ba_ref, rate_ref, gain_ref, st_ref, out_ref):
    def unit(v):
        return v * lax.rsqrt(jnp.sum(v * v, axis=-1, keepdims=True) + EPS)

    q = unit(silu(qk_ref[0])) * (128 ** -0.5)
    k = unit(silu(qk_ref[1]))
    left = jnp.concatenate([k.reshape(24, 128), q.reshape(24, 128)], axis=0)
    place = lax.broadcasted_iota(jnp.int32, (48, 128), 0) % 8
    left = jnp.concatenate([jnp.where(place == s, left, 0.0) for s in range(8)], axis=1)
    st = st_ref[...]
    right = jnp.concatenate(
        [st[:, 0].reshape(1024, 128), st[:, 1].reshape(1024, 128)], axis=1
    ).astype(BF16)
    met = jnp.dot(left.astype(BF16), right, preferred_element_type=F32)
    ba = ba_ref[...]
    kk = {(i, t): jnp.sum(k[i] * k[t], axis=-1, keepdims=True) for i in range(3) for t in range(i + 1, 3)}
    kq = {(i, t): jnp.sum(k[i] * q[t], axis=-1, keepdims=True) for i in range(3) for t in range(i, 3)}
    for j in range(2):
        lane = slice(128 * j, 128 * j + 128)
        raw = ba[:, :, 2 + j : 3 + j] + rate_ref[1:2, j : j + 1]
        decay = jnp.exp(-jnp.exp(rate_ref[0:1, j : j + 1]) * jax.nn.softplus(raw))
        beta = jax.nn.sigmoid(ba[:, :, j : j + 1])
        deltas = []
        for t in range(3):
            whole = decay[0]
            for i in range(1, t + 1):
                whole = whole * decay[i]
            recalled = whole * met[8 * t : 8 * t + 8, lane]
            readout = whole * met[24 + 8 * t : 32 + 8 * t, lane]
            fade = jnp.ones_like(whole)
            for i in range(t - 1, -1, -1):
                fade = fade * decay[i + 1]
                recalled = recalled + (fade * kk[i, t]) * deltas[i]
                readout = readout + (fade * kq[i, t]) * deltas[i]
            deltas.append(beta[t] * (silu(vz_ref[j, 0, t]) - recalled))
            readout = readout + kq[t, t] * deltas[t]
            gated = rms_scale(readout, gain_ref[0:1]) * silu(vz_ref[j, 1, t])
            out_ref[t, :, lane] = gated.astype(BF16)


def delta_steps(qk, vz, ba, rates, gain, states):
    return pl.pallas_call(
        delta_kernel,
        name="delta_steps",
        grid=(8,),
        out_shape=jax.ShapeDtypeStruct((3, 64, 256), BF16),
        in_specs=[
            pl.BlockSpec((2, 3, 8, 128), lambda g: (0, 0, g, 0)),
            pl.BlockSpec((2, 2, 3, 8, 128), lambda g: (0, 0, 0, g, 0)),
            pl.BlockSpec((3, 8, 4), lambda g: (0, g, 0)),
            pl.BlockSpec((2, 2), lambda g: (0, 0)),
            pl.BlockSpec((1, 128), lambda g: (0, 0)),
            pl.BlockSpec((8, 2, 128, 128), lambda g: (g, 0, 0, 0)),
        ],
        out_specs=pl.BlockSpec((3, 8, 256), lambda g: (0, g, 0)),
        compiler_params=pltpu.CompilerParams(vmem_limit_bytes=32 * 2**20),
    )(qk, vz, ba, rates, gain, states)


def greet_all(p):
    barrier = pltpu.get_barrier_semaphore()

    @pl.loop(1, DEVS)
    def _(i):
        pl.semaphore_signal(barrier, inc=1, device_id=spot((p + i) % DEVS), device_id_type=MESH)

    pl.semaphore_wait(barrier, DEVS - 1)


def spread(p, first, send, recv, send_sem, recv_sem):
    @pl.loop(0, 16)
    def _(i):
        to = first + i

        @pl.when(to != p)
        def _():
            pltpu.make_async_remote_copy(
                src_ref=send.at[to],
                dst_ref=recv.at[p],
                send_sem=send_sem,
                recv_sem=recv_sem,
                device_id=spot(to),
                device_id_type=MESH,
            ).start()

        @pl.when(to == p)
        def _():
            pltpu.make_async_copy(send.at[to], recv.at[p], recv_sem).start()


def take(ref, sem):
    most = ref.at[pl.ds(0, ref.shape[0] - 1)]
    pltpu.make_async_copy(most, most, sem).wait()


def slot_parts(index):
    return index // 16, (index // 4) % 4, (index // 2) % 2, index % 2


def order_matrix(flip):
    rows = lax.broadcasted_iota(jnp.int32, (256, 256), flip)
    cols = lax.broadcasted_iota(jnp.int32, (256, 256), 1 - flip)
    source, chunk, expert, rank = slot_parts(cols)
    return jnp.where(rows == chunk * 64 + expert * 32 + rank * 16 + source, 1.0, 0.0).astype(BF16)


def dispatch_kernel(
    part_ref, hid_ref, gain_ref, ids_ref, x_ref, resid_ref, slice_ref,
    rs, send, recv, psend, stacked, rs_send, rs_recv, p_send, p_recv, send_sem, recv_sem,
):
    b = lax.axis_index("batch")
    h = lax.axis_index("head")
    p = b * HEADS + h
    greet_all(p)
    for i in range(1, HEADS):
        to = (h + i) % HEADS
        pltpu.make_async_remote_copy(
            src_ref=part_ref.at[:, to], dst_ref=rs.at[h], send_sem=rs_send, recv_sem=rs_recv,
            device_id=(b, to), device_id_type=MESH,
        ).start()
    take(rs, rs_recv)
    total = part_ref[:, h].astype(F32)
    for i in range(1, HEADS):
        total = total + rs[(h + i) % HEADS].astype(F32)
    resid = (hid_ref[...].astype(F32) + total).astype(BF16)
    resid_ref[...] = resid
    post = rms_scale(resid.astype(F32), gain_ref[...].reshape(1, 1, 2048)).astype(BF16)
    for i in range(HEADS):
        psend[i] = post[:, :, 256 * i : 256 * i + 256]
    rows = post.astype(F32).reshape(24, 2048)
    blank = jnp.zeros((8, 512), F32)
    stacked[...] = jnp.concatenate(
        [v for j in range(4) for v in (rows[:, 512 * j : 512 * j + 512], blank)], axis=0
    ).astype(BF16)
    for i in range(1, HEADS):
        to = (h + i) % HEADS
        pltpu.make_async_remote_copy(
            src_ref=psend.at[to], dst_ref=slice_ref.at[h], send_sem=p_send, recv_sem=p_recv,
            device_id=(b, to), device_id_type=MESH,
        ).start()
    slice_ref[h] = psend[h]
    i0 = lax.broadcasted_iota(jnp.int32, (128, 128), 0)
    i1 = lax.broadcasted_iota(jnp.int32, (128, 128), 1)
    earlier = jnp.where((i0 // 32 == i1 // 32) & (i0 < i1), 1.0, 0.0).astype(BF16)
    row = lax.broadcasted_iota(jnp.int32, (256, 128), 0)
    lane_chunk = lax.broadcasted_iota(jnp.int32, (256, 128), 1) // 32
    owner, chunk, expert, rank = slot_parts(row)
    named = owner * 2 + expert

    @pl.loop(0, 8)
    def _(i):
        group = (p // 16 + i) % 8
        here = named + group * 32
        hot = jnp.zeros((256, 128), F32)
        for k in range(10):
            hot = hot + jnp.where(ids_ref[k : k + 1, :] == here, 1.0, 0.0)
        before = jnp.dot(hot.astype(BF16), earlier, preferred_element_type=F32)
        chosen = (before == rank.astype(F32)) & (lane_chunk == chunk)
        placing = jnp.where(chosen, hot, 0.0).astype(BF16)
        rows = jnp.dot(placing, stacked[...], preferred_element_type=F32).astype(BF16)
        send[pl.ds(group * 16, 16)] = rows.reshape(16, 16, 512)
        spread(p, group * 16, send, recv, send_sem, recv_sem)

    order = order_matrix(0)
    pltpu.make_async_copy(recv, recv, recv_sem).wait()
    for g in range(8):
        got = recv[16 * g : 16 * g + 16].reshape(256, 512)
        got = jnp.dot(order, got, preferred_element_type=F32).astype(BF16)
        for j in range(4):
            for e in range(2):
                at = j * 64 + e * 32
                x_ref[e, 32 * g : 32 * g + 32, 512 * j : 512 * j + 512] = got[at : at + 32]
    take(psend, p_recv)
    take(rs, rs_send)
    take(psend, p_send)
    take(send, send_sem)


def dispatch(part, hid, gain, ids):
    return pl.pallas_call(
        dispatch_kernel,
        name="dispatch",
        out_shape=(
            jax.ShapeDtypeStruct((2, 256, 2048), BF16),
            jax.ShapeDtypeStruct((3, 8, 2048), BF16),
            jax.ShapeDtypeStruct((HEADS, 3, 8, 256), BF16),
        ),
        in_specs=[VMEM] * 4,
        out_specs=(VMEM,) * 3,
        scratch_shapes=[
            pltpu.VMEM((HEADS, 3, 8, 2048), BF16),
            pltpu.VMEM((DEVS, 16, 512), BF16),
            pltpu.VMEM((DEVS, 16, 512), BF16),
            pltpu.VMEM((HEADS, 3, 8, 256), BF16),
            pltpu.VMEM((128, 512), BF16),
        ]
        + [pltpu.SemaphoreType.DMA(())] * 6,
        compiler_params=pltpu.CompilerParams(
            collective_id=1, has_side_effects=True, vmem_limit_bytes=40 * 2**20
        ),
    )(part, hid, gain, ids)


def return_kernel(
    y_ref, sp_ref, ids_ref, w_ref, resid_ref, down_ref, out_ref,
    send, recv, sp_recv, mids, pair, pairs, gs, gr, ms, mr, ps, pr, send_sem, recv_sem,
):
    b = lax.axis_index("batch")
    h = lax.axis_index("head")
    p = b * HEADS + h
    greet_all(p)

    def to_heads(src, dst, ssem, rsem):
        for i in range(1, HEADS):
            to = (h + i) % HEADS
            pltpu.make_async_remote_copy(
                src_ref=src(to), dst_ref=dst.at[h], send_sem=ssem, recv_sem=rsem,
                device_id=(b, to), device_id_type=MESH,
            ).start()

    to_heads(lambda to: sp_ref.at[to], sp_recv, gs, gr)
    order = order_matrix(1)

    @pl.loop(0, 8)
    def _(i):
        group = (p // 16 + i) % 8
        at = pl.multiple_of(group * 32, 32)
        rows = jnp.concatenate(
            [y_ref[e, pl.ds(at, 32), 512 * j : 512 * j + 512] for j in range(4) for e in range(2)],
            axis=0,
        )
        rows = jnp.dot(order, rows, preferred_element_type=F32).astype(BF16)
        send[pl.ds(group * 16, 16)] = rows.reshape(16, 16, 512)
        spread(p, group * 16, send, recv, send_sem, recv_sem)

    take(sp_recv, gr)
    total = sp_ref[h].astype(F32)
    for i in range(1, HEADS):
        total = total + sp_recv[(h + i) % HEADS].astype(F32)
    logit = total[:, :, 1024:1025] + total[:, :, 1025:1026]
    mid = silu(total[:, :, :512]) * total[:, :, 512:1024] * jax.nn.sigmoid(logit)
    mids[h] = mid.astype(BF16)
    to_heads(lambda to: mids.at[h], mids, ms, mr)

    i0 = lax.broadcasted_iota(jnp.int32, (128, 128), 0)
    i1 = lax.broadcasted_iota(jnp.int32, (128, 128), 1)
    earlier = jnp.where((i0 // 32 == i1 // 32) & (i1 < i0), 1.0, 0.0).astype(BF16)
    col = lax.broadcasted_iota(jnp.int32, (128, 256), 1)
    row_chunk = lax.broadcasted_iota(jnp.int32, (128, 256), 0) // 32
    owner, chunk, expert, rank = slot_parts(col)
    named = owner * 2 + expert

    def weights(g):
        here = named + g * 32
        hot = jnp.zeros((128, 256), F32)
        load = jnp.zeros((128, 256), F32)
        for k in range(10):
            same = ids_ref[:, k : k + 1] == here
            hot = hot + jnp.where(same, 1.0, 0.0)
            load = load + jnp.where(same, w_ref[:, k : k + 1], 0.0)
        before = jnp.dot(earlier, hot.astype(BF16), preferred_element_type=F32)
        load = jnp.where((before == rank.astype(F32)) & (row_chunk == chunk), load, 0.0)
        high = load.astype(BF16)
        return jnp.concatenate([high, (load - high.astype(F32)).astype(BF16)], axis=0)

    load = [weights(g) for g in range(8)]
    pltpu.make_async_copy(recv, recv, recv_sem).wait()
    acc = jnp.zeros((256, 512), F32)
    for g in range(8):
        got = recv[16 * g : 16 * g + 16].reshape(256, 512)
        acc = acc + jnp.dot(load[g], got, preferred_element_type=F32)
    acc = acc[:128] + acc[128:]
    routed = jnp.concatenate([acc[32 * j : 32 * j + 24] for j in range(4)], axis=1)
    routed = routed.reshape(3, 8, 2048).astype(BF16)
    for i in range(HEADS):
        pair[i, 0] = resid_ref[:, :, 256 * i : 256 * i + 256]
        pair[i, 1] = routed[:, :, 256 * i : 256 * i + 256]
    to_heads(lambda to: pair.at[to], pairs, ps, pr)
    pairs[h] = pair[h]
    take(mids, mr)
    every = mids[...].astype(F32).reshape(192, 512).astype(BF16)
    shared = jnp.dot(every, down_ref[...], preferred_element_type=F32).reshape(HEADS, 3, 8, 256)
    take(pairs, pr)
    for o in range(HEADS):
        both = pairs[o].astype(F32)
        out_ref[:, o] = (both[0] + shared[o] + both[1]).astype(BF16)
    take(sp_recv, gs)
    take(mids, ms)
    take(pairs, ps)
    take(send, send_sem)


def give_back(y, sp, ids, w, resid, down):
    return pl.pallas_call(
        return_kernel,
        name="give_back",
        out_shape=jax.ShapeDtypeStruct((3, HEADS, 8, 256), BF16),
        in_specs=[VMEM] * 6,
        out_specs=VMEM,
        scratch_shapes=[
            pltpu.VMEM((DEVS, 16, 512), BF16),
            pltpu.VMEM((DEVS, 16, 512), BF16),
            pltpu.VMEM((HEADS, 3, 8, 1152), BF16),
            pltpu.VMEM((HEADS, 3, 8, 512), BF16),
            pltpu.VMEM((HEADS, 2, 3, 8, 256), BF16),
            pltpu.VMEM((HEADS, 2, 3, 8, 256), BF16),
        ]
        + [pltpu.SemaphoreType.DMA(())] * 8,
        compiler_params=pltpu.CompilerParams(
            collective_id=2, has_side_effects=True, vmem_limit_bytes=40 * 2**20
        ),
    )(y, sp, ids, w, resid, down)


def shards(
    hidden_in, states, norm_in, w_qk, w_vz, w_ba, a_log, dt_bias, norm_gate, w_out, norm_post,
    shared_in, shared_gate, shared_out, expert_in, expert_out, routes, route_weight,
):
    hid = hidden_in.transpose(1, 0, 2)
    ids = routes.transpose(1, 0, 2).reshape(24, 10)
    ids = jnp.pad(ids, ((0, 8), (0, 6)), constant_values=-1)
    ids = jnp.tile(ids, (4, 1))
    load = route_weight.transpose(1, 0, 2).reshape(24, 10)
    load = jnp.tile(jnp.pad(load, ((0, 8), (0, 6))), (4, 1))
    gathered = gather_head(hid).reshape(192, 2048)
    normed = rms_scale(gathered.astype(F32), norm_in).astype(BF16)
    qk = jnp.einsum("nd,dhck->chnk", normed, w_qk, preferred_element_type=F32)
    vz = jnp.einsum("nd,dhcv->hcnv", normed, w_vz, preferred_element_type=F32)
    ba = jnp.einsum("nd,dch->nch", normed, w_ba, preferred_element_type=F32)
    gated = delta_steps(
        qk.reshape(2, 3, 64, 128),
        vz.reshape(2, 2, 3, 64, 128),
        ba.reshape(3, 64, 4),
        jnp.stack([a_log, dt_bias]),
        norm_gate.reshape(1, 128),
        states,
    )
    part = jnp.dot(
        gated.reshape(192, 256), w_out.reshape(256, 2048), preferred_element_type=F32
    ).astype(BF16)
    x, resid, slices = dispatch(
        part.reshape(3, HEADS, 8, 2048), hid, norm_post.reshape(1, 2048), ids.T
    )
    gate_up = jnp.einsum("xnd,xdgf->xngf", x, expert_in, preferred_element_type=F32)
    inner = (silu(gate_up[:, :, 0]) * gate_up[:, :, 1]).astype(BF16)
    y = jnp.einsum("xnf,xfd->xnd", inner, expert_out, preferred_element_type=F32).astype(BF16)
    slices = slices.reshape(192, 256)
    up = jnp.einsum("nd,dcf->ncf", slices, shared_in, preferred_element_type=F32)
    logit = jnp.einsum("nd,d->n", slices, shared_gate, preferred_element_type=F32)[:, None]
    high = logit.astype(BF16)
    low = (logit - high.astype(F32)).astype(BF16)
    sp = jnp.concatenate(
        [up.reshape(192, 1024).astype(BF16), high, low, jnp.zeros((192, 126), BF16)], axis=1
    )
    out = give_back(y, sp.reshape(HEADS, 3, 8, 1152), ids, load, resid, shared_out)
    return out.reshape(3, 64, 256).transpose(1, 0, 2)


def solution(mesh):
    in_specs = (
        P(("batch", "head"), None, None),
        P("batch", "head", None, None),
        P(),
        P(None, "head", None, None),
        P(None, "head", None, None),
        P(None, None, "head"),
        P("head"),
        P("head"),
        P(),
        P("head", None, None),
        P(),
        P("head", None, None),
        P("head"),
        P(None, "head"),
        P(("batch", "head"), None, None, None),
        P(("batch", "head"), None, None),
        P(("batch", "head"), None, None),
        P(("batch", "head"), None, None),
    )
    out_specs = P("batch", None, "head")
    return jax.shard_map(shards, mesh=mesh, in_specs=in_specs, out_specs=out_specs, check_vma=False)
```

profile of v0, /device:TPU:1, one launch (start us, length us, event | category | flops | bytes accessed | tf_op | source)
XLA Modules:
  0.0 143.0 jit_solution(18386268446542250841)
XLA Ops:
  0.0 13.2 %gather_input.1 = bf16[3,8,8,2048]{3,2,1,0:T(8,128)(2,1)} custom-call(bf16[3,8,2048]{2,1,0:T(8,128)(2,1)} %bitcast.92), custom_call_target="tpu_custom_call" | custom-call | tf_op jit(solution)/shard_map/gather_input/pallas_call | solution.py:76
  13.3 1.5 %multiply_reduce_fusion = f32[3,8,8]{2,1,0:T(8,128)S(1)} fusion(bf16[3,8,8,2048]{3,2,1,0:T(8,128)(2,1)} %gather_input.1), kind=kLoop, calls=%fused_computation.11 | loop fusion | flops 1179456 | bytes 787200 | tf_op jit(solution)/shard_map/reduce_sum | solution.py:21
  14.7 1.5 %multiply_convert_fusion = bf16[3,8,8,2048]{3,2,1,0:T(8,128)(2,1)S(1)} fusion(f32[2048]{0:T(1024)} %param.20, f32[3,8,8]{2,1,0:T(8,128)S(1)} %add_rsqrt_fusion, bf16[3,8,8,2048]{3,2,1,0:T(8,128)(2,1)} %gather_input.1), kind=kLoop, calls=%fused_computation.10 | loop fusion | flops 1572864 | bytes 1581824 | tf_op jit(solution)/shard_map/convert_element_type | solution.py:416
  16.2 0.9 copy-done.9
  17.1 0.4 fusion.9
  17.6 0.3 fusion.6
  17.9 0.6 fusion.3
  18.6 0.4 copy-done.10
  19.0 0.3 fusion.12.ba_ref
  19.4 3.4 %copy-done.1 = f32[64,2,128,128]{3,2,1,0:T(8,128)S(1)} copy-done((f32[64,2,128,128]{3,2,1,0:T(8,128)S(1)}, f32[64,2,128,128]{3,2,1,0:T(8,128)}, u32[]{:S(2)}) %copy-start.1) | copy-done | bytes 8388632
  22.8 3.8 %delta_steps.1 = bf16[3,64,256]{2,1,0:T(8,128)(2,1)S(1)} custom-call(f32[2,3,64,128]{3,2,1,0:T(8,128)S(1)} %bitcast.97, f32[2,2,3,64,128]{4,3,2,1,0:T(8,128)S(1)} %bitcast.89, f32[3,64,4]{2,1,0:T(8,128)S(1)} %fusion.12.ba_ref, f32[2,2]{1,0:T(2,128)S(1)} %pad_maximum_fusion.rate_ref, f32[1,128]{1,0:T(1,128)S(1)} %bitcast.99, f32[64,2,128,128]{3,2,1,0:T(8,128)S(1)} %copy-done.1), custom_call_target="tpu_custom_call" | custom-call | tf_op jit(solution)/shard_map/delta_steps/pallas_call | solution.py:132
  26.6 0.4 convolution_convert_fusion.1
  27.1 0.4 copy-done.3
  27.5 51.5 %dispatch.1 = (bf16[2,256,2048]{2,1,0:T(8,128)(2,1)S(1)}, bf16[3,8,2048]{2,1,0:T(8,128)(2,1)S(1)}, bf16[8,3,8,256]{3,2,1,0:T(8,128)(2,1)S(1)}) custom-call(bf16[3,8,8,2048]{3,2,1,0:T(8,128)(2,1)S(1)} %bitcast.86, bf16[3,8,2048]{2,1,0:T(8,128)(2,1)S(1)} %bitcast.93, f32[1,2048]{1,0:T(1,128)S(1)} %bitcast.98, s32[16,128]{1,0:T(8,128)S(1)} %copy.28.ids_ref), custom_call_target="tpu_custom_call" | custom-call | tf_op jit(solution)/shard_map/dispatch/pallas_call | solution.py:270
  79.0 5.9 %fusion = f32[2,256,2,512]{3,1,2,0:T(8,128)S(1)} fusion(bf16[2,2048,2,512]{3,2,1,0:T(2,128)(2,1)} %param.32, bf16[2,256,2048]{2,1,0:T(8,128)(2,1)S(1)} %get-tuple-element.8), kind=kOutput, calls=%fused_computation | convolution fusion | flops 2147483648 | bytes 12582912 | tf_op jit(solution)/shard_map/xnd,xdgf->xngf/dot_general | solution.py:434
  84.9 2.7 %convolution_convert_fusion.y_ref = bf16[2,256,2048]{2,1,0:T(8,128)(2,1)} fusion(bf16[2,512,2048]{2,1,0:T(8,128)(2,1)S(1)} %copy-done.18, f32[2,256,2,512]{3,1,2,0:T(8,128)S(1)} %fusion), kind=kOutput, calls=%fused_computation.2 | convolution fusion | flops 1076363264 | bytes 8388608 | tf_op jit(solution)/shard_map/xnf,xfd->xnd/dot_general | solution.py:436
  87.7 0.3 convolution_convert_fusion.2
  88.0 0.1 fusion.17
  88.1 0.3 concatenate.14
  88.4 0.2 concatenate.15
  88.7 0.1 concatenate.13.sp_ref
  88.8 1.6 %copy-done.2 = bf16[2,256,2048]{2,1,0:T(8,128)(2,1)S(1)} copy-done((bf16[2,256,2048]{2,1,0:T(8,128)(2,1)S(1)}, bf16[2,256,2048]{2,1,0:T(8,128)(2,1)}, u32[]{:S(2)}) %copy-start.2) | copy-done | bytes 2097176
  90.4 51.9 %give_back.1 = bf16[3,8,8,256]{3,2,1,0:T(8,128)(2,1)S(1)} custom-call(bf16[2,256,2048]{2,1,0:T(8,128)(2,1)S(1)} %copy-done.2, bf16[8,3,8,1152]{3,2,1,0:T(8,128)(2,1)S(1)} %concatenate.13.sp_ref, s32[128,16]{1,0:T(8,128)S(1)} %bitcast.88, f32[128,16]{1,0:T(8,128)S(1)} %bitcast.96, bf16[3,8,2048]{2,1,0:T(8,128)(2,1)S(1)} %get-tuple-element.10.resid_ref, ...), custom_call_target="tpu_custom_call" | custom-call | tf_op jit(solution)/shard_map/give_back/pallas_call | solution.py:384
  142.3 0.6 copy.45
  (50 shorter events, 0.5 us)
Async XLA Ops:
  0.0 17.9 %copy-start = (bf16[2048,2,2,128]{3,2,1,0:T(2,128)(2,1)S(1)}, bf16[2048,2,2,128]{3,2,1,0:T(2,128)(2,1)}, u32[]{:S(2)}) copy-start(bf16[2048,2,2,128]{3,2,1,0:T(2,128)(2,1)} %param.22) | copy-start | bytes 6291460
  13.3 3.9 %copy-start.19 = (bf16[2048,1,2,128]{3,2,1,0:T(2,128)(2,1)S(1)}, bf16[2048,1,2,128]{3,2,1,0:T(2,128)(2,1)}, u32[]{:S(2)}) copy-start(bf16[2048,1,2,128]{3,2,1,0:T(2,128)(2,1)} %param.21) | copy-start | bytes 3145732
  14.7 2.9 %copy-start.7 = (bf16[3,8,8,2048]{3,2,1,0:T(8,128)(2,1)S(1)}, bf16[3,8,8,2048]{3,2,1,0:T(8,128)(2,1)}, u32[]{:S(2)}) copy-start(bf16[3,8,8,2048]{3,2,1,0:T(8,128)(2,1)} %gather_input.1) | copy-start | bytes 2359300
  14.7 2.9 %copy-start.12 = (f32[2048]{0:T(1024)S(1)}, f32[2048]{0:T(1024)}, u32[]{:S(2)}) copy-start(f32[2048]{0:T(1024)} %param.20) | copy-start | bytes 24580
  16.2 0.9 copy-start.9
  17.9 0.7 copy-start.13
  17.9 1.1 copy-start.10
  17.9 1.5 %copy-start.16 = (f32[2]{0:T(128)S(1)}, f32[2]{0:T(128)}, u32[]{:S(2)}) copy-start(f32[2]{0:T(128)} %param.25) | copy-start | bytes 28
  17.9 1.5 %copy-start.17 = (f32[2]{0:T(128)S(1)}, f32[2]{0:T(128)}, u32[]{:S(2)}) copy-start(f32[2]{0:T(128)} %param.24) | copy-start | bytes 28
  17.9 1.5 %copy-start.6 = (f32[128]{0:T(128)S(1)}, f32[128]{0:T(128)}, u32[]{:S(2)}) copy-start(f32[128]{0:T(128)} %param.26) | copy-start | bytes 1540
  19.4 3.4 %copy-start.1 = (f32[64,2,128,128]{3,2,1,0:T(8,128)S(1)}, f32[64,2,128,128]{3,2,1,0:T(8,128)}, u32[]{:S(2)}) copy-start(f32[64,2,128,128]{3,2,1,0:T(8,128)} %st_ref.1) | copy-start | bytes 25165828
  22.8 3.8 %copy-start.8 = (bf16[2,128,2048]{2,1,0:T(8,128)(2,1)S(1)}, bf16[2,128,2048]{2,1,0:T(8,128)(2,1)}, u32[]{:S(2)}) copy-start(bf16[2,128,2048]{2,1,0:T(8,128)(2,1)} %param.27) | copy-start | bytes 3145732
  22.8 4.2 %copy-start.14 = (s32[8,3,10]{2,0,1:T(8,128)S(1)}, s32[8,3,10]{2,0,1:T(8,128)}, u32[]{:S(2)}) copy-start(s32[8,3,10]{2,0,1:T(8,128)} %param.34) | copy-start | bytes 2884
  26.6 0.9 copy-start.3
  26.6 0.9 copy-start.5
  79.0 5.9 %copy-start.18 = (bf16[2,512,2048]{2,1,0:T(8,128)(2,1)S(1)}, bf16[2,512,2048]{2,1,0:T(8,128)(2,1)}, u32[]{:S(2)}) copy-start(bf16[2,512,2048]{2,1,0:T(8,128)(2,1)} %param.33) | copy-start | bytes 12582916
  84.9 2.7 %copy-start.11 = (bf16[256,2,512]{2,1,0:T(2,128)(2,1)S(1)}, bf16[256,2,512]{2,1,0:T(2,128)(2,1)}, u32[]{:S(2)}) copy-start(bf16[256,2,512]{2,1,0:T(2,128)(2,1)} %param.29) | copy-start | bytes 1572868
  84.9 3.1 %copy-start.20 = (bf16[256]{0:T(256)(128)(2,1)S(1)}, bf16[256]{0:T(256)(128)(2,1)}, u32[]{:S(2)}) copy-start(bf16[256]{0:T(256)(128)(2,1)} %param.30) | copy-start | bytes 1540
  87.6 1.2 copy-start.15
  87.6 1.2 copy-start.4
  88.8 1.6 %copy-start.2 = (bf16[2,256,2048]{2,1,0:T(8,128)(2,1)S(1)}, bf16[2,256,2048]{2,1,0:T(8,128)(2,1)}, u32[]{:S(2)}) copy-start(bf16[2,256,2048]{2,1,0:T(8,128)(2,1)} %convolution_convert_fusion.y_ref) | copy-start | bytes 6291460
where the time goes:
time: 143 us
  Pallas kernels  120 us (84%)
  matrix products  10.6 us (7%)
  local copies, waits for them, and re-layouts  8.38 us (6%)
  other arithmetic  3.2 us (2%)
    pallas_call x1, Pallas kernels, give_back(): pl.pallas_call(return_kernel, name='give_back', out_shape=jax.ShapeDtypeS...  51.9 us
    pallas_call x1, Pallas kernels, dispatch(): pl.pallas_call(dispatch_kernel, name='dispatch', out_shape=(jax.ShapeDtyp...  51.5 us
    pallas_call x1, Pallas kernels, gather_head(): pl.pallas_call(gather_kernel, name='gather_input', out_shape=jax.ShapeDty...  13.2 us
    unnamed x45, local copies, waits for them, and re-layouts  7.56 us
    dot_general x1, matrix products, shards(): jnp.einsum('xnd,xdgf->xngf', x, expert_in, preferred_element_type=F32)  5.86 us
    pallas_call x1, Pallas kernels, delta_steps(): pl.pallas_call(delta_kernel, name='delta_steps', grid=(8,), out_shape=jax...  3.77 us

commit v1 on v0

--- a/solution.py
+++ b/solution.py
@@ -194,111 +194,35 @@
     return jnp.where(rows == chunk * 64 + expert * 32 + rank * 16 + source, 1.0, 0.0).astype(BF16)
 
 
-def dispatch_kernel(
-    part_ref, hid_ref, gain_ref, ids_ref, x_ref, resid_ref, slice_ref,
-    rs, send, recv, psend, stacked, rs_send, rs_recv, p_send, p_recv, send_sem, recv_sem,
+def part_rows(raw, wide, blocks):
+    rows = lax.broadcasted_iota(jnp.int32, (256, 256), 0)
+    cols = lax.broadcasted_iota(jnp.int32, (256, 256), 1)
+    order = jnp.where(cols == (rows % 32) * 8 + rows // 32, 1.0, 0.0).astype(BF16)
+
+    @pl.loop(0, blocks)
+    def _(i):
+        at = pl.multiple_of(i * 512, 512)
+        to = pl.multiple_of(i * 64, 64)
+        pair = jnp.concatenate([raw[pl.ds(at, 256)], raw[pl.ds(at + 256, 256)]], axis=1)
+        got = jnp.dot(order, pair, preferred_element_type=F32).astype(BF16)
+        for s in range(8):
+            lane = (s % 2) * 512 + (s // 2) * 128
+            part = got[32 * s : 32 * s + 32]
+            wide[pl.ds(to, 32), lane : lane + 128] = part[:, :128]
+            wide[pl.ds(to + 32, 32), lane : lane + 128] = part[:, 128:]
+
+
+def moe_kernel(
+    part_ref, hid_ref, gain_ref, idt_ref, ids_ref, w_ref, sraw_ref, sgate_ref, down_ref, win_ref, wout_ref,
+    out_ref,
+    rs, send, recv, psend, slices, stacked, placing, load, raw, win, wout, swin, xs, ys,
+    back, home, sp, sp_recv, mids, pair, pairs,
+    rs_s, rs_r, p_s, p_r, d_s, d_r, b_s, b_r, g_s, g_r, m_s, m_r, q_s, q_r, win_sem, wout_sem,
 ):
     b = lax.axis_index("batch")
     h = lax.axis_index("head")
     p = b * HEADS + h
-    greet_all(p)
-    for i in range(1, HEADS):
-        to = (h + i) % HEADS
-        pltpu.make_async_remote_copy(
-            src_ref=part_ref.at[:, to], dst_ref=rs.at[h], send_sem=rs_send, recv_sem=rs_recv,
-            device_id=(b, to), device_id_type=MESH,
-        ).start()
-    take(rs, rs_recv)
-    total = part_ref[:, h].astype(F32)
-    for i in range(1, HEADS):
-        total = total + rs[(h + i) % HEADS].astype(F32)
-    resid = (hid_ref[...].astype(F32) + total).astype(BF16)
-    resid_ref[...] = resid
-    post = rms_scale(resid.astype(F32), gain_ref[...].reshape(1, 1, 2048)).astype(BF16)
-    for i in range(HEADS):
-        psend[i] = post[:, :, 256 * i : 256 * i + 256]
-    rows = post.astype(F32).reshape(24, 2048)
-    blank = jnp.zeros((8, 512), F32)
-    stacked[...] = jnp.concatenate(
-        [v for j in range(4) for v in (rows[:, 512 * j : 512 * j + 512], blank)], axis=0
-    ).astype(BF16)
-    for i in range(1, HEADS):
-        to = (h + i) % HEADS
-        pltpu.make_async_remote_copy(
-            src_ref=psend.at[to], dst_ref=slice_ref.at[h], send_sem=p_send, recv_sem=p_recv,
-            device_id=(b, to), device_id_type=MESH,
-        ).start()
-    slice_ref[h] = psend[h]
-    i0 = lax.broadcasted_iota(jnp.int32, (128, 128), 0)
-    i1 = lax.broadcasted_iota(jnp.int32, (128, 128), 1)
-    earlier = jnp.where((i0 // 32 == i1 // 32) & (i0 < i1), 1.0, 0.0).astype(BF16)
-    row = lax.broadcasted_iota(jnp.int32, (256, 128), 0)
-    lane_chunk = lax.broadcasted_iota(jnp.int32, (256, 128), 1) // 32
-    owner, chunk, expert, rank = slot_parts(row)
-    named = owner * 2 + expert
-
-    @pl.loop(0, 8)
-    def _(i):
-        group = (p // 16 + i) % 8
-        here = named + group * 32
-        hot = jnp.zeros((256, 128), F32)
-        for k in range(10):
-            hot = hot + jnp.where(ids_ref[k : k + 1, :] == here, 1.0, 0.0)
-        before = jnp.dot(hot.astype(BF16), earlier, preferred_element_type=F32)
-        chosen = (before == rank.astype(F32)) & (lane_chunk == chunk)
-        placing = jnp.where(chosen, hot, 0.0).astype(BF16)
-        rows = jnp.dot(placing, stacked[...], preferred_element_type=F32).astype(BF16)
-        send[pl.ds(group * 16, 16)] = rows.reshape(16, 16, 512)
-        spread(p, group * 16, send, recv, send_sem, recv_sem)
-
-    order = order_matrix(0)
-    pltpu.make_async_copy(recv, recv, recv_sem).wait()
-    for g in range(8):
-        got = recv[16 * g : 16 * g + 16].reshape(256, 512)
-        got = jnp.dot(order, got, preferred_element_type=F32).astype(BF16)
-        for j in range(4):
-            for e in range(2):
-                at = j * 64 + e * 32
-                x_ref[e, 32 * g : 32 * g + 32, 512 * j : 512 * j + 512] = got[at : at + 32]
-    take(psend, p_recv)
-    take(rs, rs_send)
-    take(psend, p_send)
-    take(send, send_sem)
-
-
-def dispatch(part, hid, gain, ids):
-    return pl.pallas_call(
-        dispatch_kernel,
-        name="dispatch",
-        out_shape=(
-            jax.ShapeDtypeStruct((2, 256, 2048), BF16),
-            jax.ShapeDtypeStruct((3, 8, 2048), BF16),
-            jax.ShapeDtypeStruct((HEADS, 3, 8, 256), BF16),
-        ),
-        in_specs=[VMEM] * 4,
-        out_specs=(VMEM,) * 3,
-        scratch_shapes=[
-            pltpu.VMEM((HEADS, 3, 8, 2048), BF16),
-            pltpu.VMEM((DEVS, 16, 512), BF16),
-            pltpu.VMEM((DEVS, 16, 512), BF16),
-            pltpu.VMEM((HEADS, 3, 8, 256), BF16),
-            pltpu.VMEM((128, 512), BF16),
-        ]
-        + [pltpu.SemaphoreType.DMA(())] * 6,
-        compiler_params=pltpu.CompilerParams(
-            collective_id=1, has_side_effects=True, vmem_limit_bytes=40 * 2**20
-        ),
-    )(part, hid, gain, ids)
-
-
-def return_kernel(
-    y_ref, sp_ref, ids_ref, w_ref, resid_ref, down_ref, out_ref,
-    send, recv, sp_recv, mids, pair, pairs, gs, gr, ms, mr, ps, pr, send_sem, recv_sem,
-):
-    b = lax.axis_index("batch")
-    h = lax.axis_index("head")
-    p = b * HEADS + h
-    greet_all(p)
+    mine = p // 16
 
     def to_heads(src, dst, ssem, rsem):
         for i in range(1, HEADS):
@@ -308,98 +232,212 @@
                 device_id=(b, to), device_id_type=MESH,
             ).start()
 
-    to_heads(lambda to: sp_ref.at[to], sp_recv, gs, gr)
-    order = order_matrix(1)
+    win_copy = pltpu.make_async_copy(win_ref, raw, win_sem)
+    win_copy.start()
+    wout_copy = pltpu.make_async_copy(wout_ref, wout, wout_sem)
+    wout_copy.start()
+    greet_all(p)
+    to_heads(lambda to: part_ref.at[:, to], rs, rs_s, rs_r)
+
+    i0 = lax.broadcasted_iota(jnp.int32, (128, 128), 0)
+    i1 = lax.broadcasted_iota(jnp.int32, (128, 128), 1)
+    earlier = jnp.where((i0 // 32 == i1 // 32) & (i0 < i1), 1.0, 0.0).astype(BF16)
+    later = jnp.where((i0 // 32 == i1 // 32) & (i1 < i0), 1.0, 0.0).astype(BF16)
+    lane_chunk = lax.broadcasted_iota(jnp.int32, (256, 128), 1) // 32
+    owner, chunk, expert, rank = slot_parts(lax.broadcasted_iota(jnp.int32, (256, 128), 0))
+    named = owner * 2 + expert
+
+    @pl.loop(0, 8)
+    def _(g):
+        here = named + g * 32
+        hot = jnp.zeros((256, 128), F32)
+        for k in range(10):
+            hot = hot + jnp.where(idt_ref[k : k + 1, :] == here, 1.0, 0.0)
+        before = jnp.dot(hot.astype(BF16), earlier, preferred_element_type=F32)
+        chosen = (before == rank.astype(F32)) & (lane_chunk == chunk)
+        placing[g] = jnp.where(chosen, hot, 0.0).astype(BF16)
+
+    part_rows(sraw_ref, swin, 4)
+    win_copy.wait()
+    part_rows(raw, win, 64)
+
+    take(rs, rs_r)
+    total = part_ref[:, h].astype(F32)
+    for i in range(1, HEADS):
+        total = total + rs[(h + i) % HEADS].astype(F32)
+    resid = (hid_ref[...].astype(F32) + total).astype(BF16)
+    post = rms_scale(resid.astype(F32), gain_ref[...].reshape(1, 1, 2048)).astype(BF16)
+    for i in range(HEADS):
+        psend[i] = post[:, :, 256 * i : 256 * i + 256]
+        pair[i, 0] = resid[:, :, 256 * i : 256 * i + 256]
+    to_heads(lambda to: psend.at[to], slices, p_s, p_r)
+    slices[h] = psend[h]
+    rows = post.astype(F32).reshape(24, 2048)
+    blank = jnp.zeros((8, 512), F32)
+    stacked[...] = jnp.concatenate(
+        [v for j in range(4) for v in (rows[:, 512 * j : 512 * j + 512], blank)], axis=0
+    ).astype(BF16)
 
     @pl.loop(0, 8)
     def _(i):
-        group = (p // 16 + i) % 8
-        at = pl.multiple_of(group * 32, 32)
-        rows = jnp.concatenate(
-            [y_ref[e, pl.ds(at, 32), 512 * j : 512 * j + 512] for j in range(4) for e in range(2)],
-            axis=0,
-        )
-        rows = jnp.dot(order, rows, preferred_element_type=F32).astype(BF16)
+        group = (mine + i) % 8
+        rows = jnp.dot(placing[group], stacked[...], preferred_element_type=F32).astype(BF16)
         send[pl.ds(group * 16, 16)] = rows.reshape(16, 16, 512)
-        spread(p, group * 16, send, recv, send_sem, recv_sem)
-
-    take(sp_recv, gr)
-    total = sp_ref[h].astype(F32)
-    for i in range(1, HEADS):
-        total = total + sp_recv[(h + i) % HEADS].astype(F32)
-    logit = total[:, :, 1024:1025] + total[:, :, 1025:1026]
-    mid = silu(total[:, :, :512]) * total[:, :, 512:1024] * jax.nn.sigmoid(logit)
-    mids[h] = mid.astype(BF16)
-    to_heads(lambda to: mids.at[h], mids, ms, mr)
-
-    i0 = lax.broadcasted_iota(jnp.int32, (128, 128), 0)
-    i1 = lax.broadcasted_iota(jnp.int32, (128, 128), 1)
-    earlier = jnp.where((i0 // 32 == i1 // 32) & (i1 < i0), 1.0, 0.0).astype(BF16)
-    col = lax.broadcasted_iota(jnp.int32, (128, 256), 1)
+        spread(p, group * 16, send, recv, d_s, d_r.at[mine])
+
+    take(psend, p_r)
+    every = slices[...].astype(F32).reshape(192, 256)
+    up = jnp.dot(every.astype(BF16), swin[...], preferred_element_type=F32)
+    logit = jnp.sum(every * sgate_ref[...].astype(F32), axis=-1, keepdims=True)
+    high = logit.astype(BF16).astype(F32)
+    zero = jnp.zeros((192, 126), F32)
+    sp[...] = (
+        jnp.concatenate([up, high, logit - high, zero], axis=1).astype(BF16).reshape(HEADS, 3, 8, 1152)
+    )
+    to_heads(lambda to: sp.at[to], sp_recv, g_s, g_r)
+
     row_chunk = lax.broadcasted_iota(jnp.int32, (128, 256), 0) // 32
-    owner, chunk, expert, rank = slot_parts(col)
-    named = owner * 2 + expert
-
-    def weights(g):
-        here = named + g * 32
+    owner2, chunk2, expert2, rank2 = slot_parts(lax.broadcasted_iota(jnp.int32, (128, 256), 1))
+    named2 = owner2 * 2 + expert2
+
+    @pl.loop(0, 8)
+    def _(g):
+        here = named2 + g * 32
         hot = jnp.zeros((128, 256), F32)
-        load = jnp.zeros((128, 256), F32)
+        heavy = jnp.zeros((128, 256), F32)
         for k in range(10):
             same = ids_ref[:, k : k + 1] == here
             hot = hot + jnp.where(same, 1.0, 0.0)
-            load = load + jnp.where(same, w_ref[:, k : k + 1], 0.0)
-        before = jnp.dot(earlier, hot.astype(BF16), preferred_element_type=F32)
-        load = jnp.where((before == rank.astype(F32)) & (row_chunk == chunk), load, 0.0)
-        high = load.astype(BF16)
-        return jnp.concatenate([high, (load - high.astype(F32)).astype(BF16)], axis=0)
-
-    load = [weights(g) for g in range(8)]
-    pltpu.make_async_copy(recv, recv, recv_sem).wait()
+            heavy = heavy + jnp.where(same, w_ref[:, k : k + 1], 0.0)
+        before = jnp.dot(later, hot.astype(BF16), preferred_element_type=F32)
+        heavy = jnp.where((before == rank2.astype(F32)) & (row_chunk == chunk2), heavy, 0.0)
+        top = heavy.astype(BF16)
+        load[g, :128] = top
+        load[g, 128:] = (heavy - top.astype(F32)).astype(BF16)
+
+    wout_copy.wait()
+    order = order_matrix(0)
+    undo = order_matrix(1)
+    for half in range(2):
+        @pl.loop(0, 4)
+        def _(i):
+            group = (mine + 8 - (4 * half + i)) % 8
+            blocks = recv.at[pl.ds(group * 16, 16)]
+            pltpu.make_async_copy(blocks, blocks, d_r.at[group]).wait()
+            got = recv[pl.ds(group * 16, 16)].reshape(256, 512)
+            got = jnp.dot(order, got, preferred_element_type=F32).astype(BF16)
+            to = pl.multiple_of(i * 32, 32)
+            for j in range(4):
+                for e in range(2):
+                    at = j * 64 + e * 32
+                    xs[e, pl.ds(to, 32), 512 * j : 512 * j + 512] = got[at : at + 32]
+
+        @pl.loop(0, 2)
+        def _(e):
+            inner = []
+            for n in range(2):
+                lane = slice(256 * n, 256 * n + 256)
+                lane2 = slice(512 + 256 * n, 768 + 256 * n)
+                gate = jnp.dot(xs[e], win[pl.ds(e * 2048, 2048), lane], preferred_element_type=F32)
+                more = jnp.dot(xs[e], win[pl.ds(e * 2048, 2048), lane2], preferred_element_type=F32)
+                inner.append((silu(gate) * more).astype(BF16))
+            inner = jnp.concatenate(inner, axis=1)
+            for j in range(4):
+                lane = slice(512 * j, 512 * j + 512)
+                ys[e, :, lane] = jnp.dot(inner, wout[e, :, lane], preferred_element_type=F32).astype(BF16)
+
+        @pl.loop(0, 4)
+        def _(i):
+            group = (mine + 8 - (4 * half + i)) % 8
+            at = pl.multiple_of(i * 32, 32)
+            rows = jnp.concatenate(
+                [ys[e, pl.ds(at, 32), 512 * j : 512 * j + 512] for j in range(4) for e in range(2)],
+                axis=0,
+            )
+            rows = jnp.dot(undo, rows, preferred_element_type=F32).astype(BF16)
+            back[pl.ds(group * 16, 16)] = rows.reshape(16, 16, 512)
+            spread(p, group * 16, back, home, b_s, b_r)
+
+        if half == 0:
+            take(sp_recv, g_r)
+            total = sp[h].astype(F32)
+            for i in range(1, HEADS):
+                total = total + sp_recv[(h + i) % HEADS].astype(F32)
+            logit = total[:, :, 1024:1025] + total[:, :, 1025:1026]
+            mid = silu(total[:, :, :512]) * total[:, :, 512:1024] * jax.nn.sigmoid(logit)
+            mids[h] = mid.astype(BF16)
+            to_heads(lambda to: mids.at[h], mids, m_s, m_r)
+
+    take(mids, m_r)
+    every = mids[...].astype(F32).reshape(192, 512).astype(BF16)
+    shared = jnp.dot(every, down_ref[...], preferred_element_type=F32).reshape(HEADS, 3, 8, 256)
+    pltpu.make_async_copy(home, home, b_r).wait()
     acc = jnp.zeros((256, 512), F32)
     for g in range(8):
-        got = recv[16 * g : 16 * g + 16].reshape(256, 512)
+        got = home[16 * g : 16 * g + 16].reshape(256, 512)
         acc = acc + jnp.dot(load[g], got, preferred_element_type=F32)
     acc = acc[:128] + acc[128:]
     routed = jnp.concatenate([acc[32 * j : 32 * j + 24] for j in range(4)], axis=1)
     routed = routed.reshape(3, 8, 2048).astype(BF16)
     for i in range(HEADS):
-        pair[i, 0] = resid_ref[:, :, 256 * i : 256 * i + 256]
         pair[i, 1] = routed[:, :, 256 * i : 256 * i + 256]
-    to_heads(lambda to: pair.at[to], pairs, ps, pr)
+    to_heads(lambda to: pair.at[to], pairs, q_s, q_r)
     pairs[h] = pair[h]
-    take(mids, mr)
-    every = mids[...].astype(F32).reshape(192, 512).astype(BF16)
-    shared = jnp.dot(every, down_ref[...], preferred_element_type=F32).reshape(HEADS, 3, 8, 256)
-    take(pairs, pr)
+    take(pairs, q_r)
     for o in range(HEADS):
         both = pairs[o].astype(F32)
         out_ref[:, o] = (both[0] + shared[o] + both[1]).astype(BF16)
-    take(sp_recv, gs)
-    take(mids, ms)
-    take(pairs, ps)
-    take(send, send_sem)
-
-
-def give_back(y, sp, ids, w, resid, down):
+    take(rs, rs_s)
+    take(psend, p_s)
+    take(send, d_s)
+    take(sp, g_s)
+    take(mids, m_s)
+    take(back, b_s)
+    take(pairs, q_s)
+
+
+def moe(*args):
+    any_place = pl.BlockSpec(memory_space=pl.ANY)
     return pl.pallas_call(
-        return_kernel,
-        name="give_back",
+        moe_kernel,
+        name="moe",
         out_shape=jax.ShapeDtypeStruct((3, HEADS, 8, 256), BF16),
-        in_specs=[VMEM] * 6,
+        in_specs=[VMEM] * 9 + [any_place] * 2,
         out_specs=VMEM,
         scratch_shapes=[
+            pltpu.VMEM((HEADS, 3, 8, 2048), BF16),
             pltpu.VMEM((DEVS, 16, 512), BF16),
             pltpu.VMEM((DEVS, 16, 512), BF16),
+            pltpu.VMEM((HEADS, 3, 8, 256), BF16),
+            pltpu.VMEM((HEADS, 3, 8, 256), BF16),
+            pltpu.VMEM((128, 512), BF16),
+            pltpu.VMEM((8, 256, 128), BF16),
+            pltpu.VMEM((8, 256, 256), BF16),
+            pltpu.VMEM((32768, 128), BF16),
+            pltpu.VMEM((4096, 1024), BF16),
+            pltpu.VMEM((2, 512, 2048), BF16),
+            pltpu.VMEM((256, 1024), BF16),
+            pltpu.VMEM((2, 128, 2048), BF16),
+            pltpu.VMEM((2, 128, 2048), BF16),
+            pltpu.VMEM((DEVS, 16, 512), BF16),
+            pltpu.VMEM((DEVS, 16, 512), BF16),
+            pltpu.VMEM((HEADS, 3, 8, 1152), BF16),
             pltpu.VMEM((HEADS, 3, 8, 1152), BF16),
             pltpu.VMEM((HEADS, 3, 8, 512), BF16),
             pltpu.VMEM((HEADS, 2, 3, 8, 256), BF16),
             pltpu.VMEM((HEADS, 2, 3, 8, 256), BF16),
         ]
-        + [pltpu.SemaphoreType.DMA(())] * 8,
+        + [pltpu.SemaphoreType.DMA(())] * 5
+        + [pltpu.SemaphoreType.DMA((8,))]
+        + [pltpu.SemaphoreType.DMA(())] * 10,
         compiler_params=pltpu.CompilerParams(
-            collective_id=2, has_side_effects=True, vmem_limit_bytes=40 * 2**20
+            collective_id=1, has_side_effects=True, vmem_limit_bytes=56 * 2**20
         ),
-    )(y, sp, ids, w, resid, down)
+    )(*args)
+
+
+def column_rows(w):
+    return w.reshape(-1, 2, 4, 128).transpose(0, 2, 1, 3).reshape(-1, 128)
 
 
 def shards(
@@ -428,21 +466,19 @@
     part = jnp.dot(
         gated.reshape(192, 256), w_out.reshape(256, 2048), preferred_element_type=F32
     ).astype(BF16)
-    x, resid, slices = dispatch(
-        part.reshape(3, HEADS, 8, 2048), hid, norm_post.reshape(1, 2048), ids.T
+    out = moe(
+        part.reshape(3, HEADS, 8, 2048),
+        hid,
+        norm_post.reshape(1, 2048),
+        ids.T,
+        ids,
+        load,
+        column_rows(shared_in),
+        shared_gate.reshape(1, 256),
+        shared_out,
+        column_rows(expert_in),
+        expert_out,
     )
-    gate_up = jnp.einsum("xnd,xdgf->xngf", x, expert_in, preferred_element_type=F32)
-    inner = (silu(gate_up[:, :, 0]) * gate_up[:, :, 1]).astype(BF16)
-    y = jnp.einsum("xnf,xfd->xnd", inner, expert_out, preferred_element_type=F32).astype(BF16)
-    slices = slices.reshape(192, 256)
-    up = jnp.einsum("nd,dcf->ncf", slices, shared_in, preferred_element_type=F32)
-    logit = jnp.einsum("nd,d->n", slices, shared_gate, preferred_element_type=F32)[:, None]
-    high = logit.astype(BF16)
-    low = (logit - high.astype(F32)).astype(BF16)
-    sp = jnp.concatenate(
-        [up.reshape(192, 1024).astype(BF16), high, low, jnp.zeros((192, 126), BF16)], axis=1
-    )
-    out = give_back(y, sp.reshape(HEADS, 3, 8, 1152), ids, load, resid, shared_out)
     return out.reshape(3, 64, 256).transpose(1, 0, 2)
 
 

time: 143 us -> 132 us (0.923)
  matrix products: 10.6 us -> 3.7 us
  Pallas kernels: 120 us -> 117 us
    dot_general x4 -> x0, matrix products: 8.96 us -> none  [the longest x1 5.86 us: shards(): jnp.einsum('xnd,xdgf->xngf', x, expert_in, preferred_element_type=F32)]
    pallas_call x2 -> x1, Pallas kernels: 103 us -> 100 us  [moe(): pl.pallas_call(moe_kernel, name='moe', out_shape=jax.ShapeDtypeStruct((3,...]
    unnamed x45 -> x31, local copies, waits for them, and re-layouts: 7.56 us -> 5.93 us
where the time goes in v1:
time: 132 us
  Pallas kernels  117 us (89%)
  local copies, waits for them, and re-layouts  7.92 us (6%)
  matrix products  3.7 us (3%)
  other arithmetic  3.12 us (2%)
    pallas_call x1, Pallas kernels, moe(): pl.pallas_call(moe_kernel, name='moe', out_shape=jax.ShapeDtypeStruct((3,...  100 us
    pallas_call x1, Pallas kernels, gather_head(): pl.pallas_call(gather_kernel, name='gather_input', out_shape=jax.ShapeDty...  13.3 us
    unnamed x31, local copies, waits for them, and re-layouts  5.93 us
    pallas_call x1, Pallas kernels, delta_steps(): pl.pallas_call(delta_kernel, name='delta_steps', grid=(8,), out_shape=jax...  3.77 us

profile of v1, /device:TPU:1, one launch (start us, length us, event | category | flops | bytes accessed | tf_op | source)
XLA Modules:
  0.0 132.1 jit_solution(14214869587047702240)
XLA Ops:
  0.0 13.3 %gather_input.1 = bf16[3,8,8,2048]{3,2,1,0:T(8,128)(2,1)} custom-call(bf16[3,8,2048]{2,1,0:T(8,128)(2,1)} %bitcast.75), custom_call_target="tpu_custom_call" | custom-call | tf_op jit(solution)/shard_map/gather_input/pallas_call | solution.py:76
  13.3 0.0 copy-start.13
  13.3 1.5 %multiply_reduce_fusion = f32[3,8,8]{2,1,0:T(8,128)S(1)} fusion(bf16[3,8,8,2048]{3,2,1,0:T(8,128)(2,1)} %gather_input.1), kind=kLoop, calls=%fused_computation.7 | loop fusion | flops 1179456 | bytes 787200 | tf_op jit(solution)/shard_map/reduce_sum | solution.py:21
  14.8 0.0 copy-start.8
  14.8 1.4 %multiply_convert_fusion = bf16[3,8,8,2048]{3,2,1,0:T(8,128)(2,1)S(1)} fusion(f32[2048]{0:T(1024)S(1)} %copy-done.7, f32[3,8,8]{2,1,0:T(8,128)S(1)} %add_rsqrt_fusion, bf16[3,8,8,2048]{3,2,1,0:T(8,128)(2,1)} %gather_input.1), kind=kLoop, calls=%fused_computation.6 | loop fusion | flops 1572864 | bytes 1581824 | tf_op jit(solution)/shard_map/convert_element_type | solution.py:454
  16.2 0.9 copy-done.5
  17.1 0.4 fusion.4
  17.5 1.5 %fusion.7.ba_ref = f32[3,64,4]{2,1,0:T(8,128)S(1)} fusion(bf16[4,2048,1]{1,0,2:T(4,128)(2,1)S(1)} %reshape.134, bf16[3,8,8,2048]{3,2,1,0:T(8,128)(2,1)} %copy-done.5), kind=kOutput, calls=%fused_computation.11 | convolution fusion | flops 3145728 | bytes 805888 | tf_op jit(solution)/shard_map/nd,dch->nch/dot_general | solution.py:457
  19.0 0.1 rsqrt.15
  19.1 0.3 fusion.3
  19.3 0.0 copy-start.12
  19.3 0.0 copy-start.2
  19.4 0.6 fusion
  19.9 0.0 copy-done.11
  20.0 0.0 copy-done.12
  20.0 0.0 copy-done.2
  20.0 3.4 %copy-done.1 = f32[64,2,128,128]{3,2,1,0:T(8,128)S(1)} copy-done((f32[64,2,128,128]{3,2,1,0:T(8,128)S(1)}, f32[64,2,128,128]{3,2,1,0:T(8,128)}, u32[]{:S(2)}) %copy-start.1) | copy-done | bytes 8388632
  23.4 3.8 %delta_steps.1 = bf16[3,64,256]{2,1,0:T(8,128)(2,1)S(1)} custom-call(f32[2,3,64,128]{3,2,1,0:T(8,128)S(1)} %bitcast.66, f32[2,2,3,64,128]{4,3,2,1,0:T(8,128)S(1)} %bitcast.64, f32[3,64,4]{2,1,0:T(8,128)S(1)} %fusion.7.ba_ref, f32[2,2]{1,0:T(2,128)S(1)} %pad_maximum_fusion.rate_ref, f32[1,128]{1,0:T(1,128)S(1)} %bitcast.67, f32[64,2,128,128]{3,2,1,0:T(8,128)S(1)} %copy-done.1), custom_call_target="tpu_custom_call" | custom-call | tf_op jit(solution)/shard_map/delta_steps/pallas_call | solution.py:132
  27.2 1.3 convolution_convert_fusion
  28.5 0.7 copy.24.idt_ref
  29.2 0.6 tile.20
  29.8 0.6 reshape.127.sgate_ref
  30.4 100.2 %moe.1 = bf16[3,8,8,256]{3,2,1,0:T(8,128)(2,1)} custom-call(bf16[3,8,8,2048]{3,2,1,0:T(8,128)(2,1)} %bitcast.69, bf16[3,8,2048]{2,1,0:T(8,128)(2,1)} %bitcast.76, f32[1,2048]{1,0:T(1,128)} %bitcast.82, s32[16,128]{1,0:T(8,128)} %copy.24.idt_ref, s32[128,16]{1,0:T(8,128)} %bitcast.73, f32[128,16]{1,0:T(8,128)} %bitcast.78, bf16[2048,128]{1,0:T(8,128)(2,1)} %bitcast.74, ...), custom_call_target="tpu_custom_call" | custom-call | tf_op jit(solution)/shard_map/moe/pallas_call | solution.py:401
  130.6 1.5 %copy.32 = bf16[64,3,256]{2,0,1:T(8,128)(2,1)} copy(bf16[64,3,256]{2,0,1:T(8,128)(2,1)} %bitcast.77) | data formatting | bytes 196608
  (27 shorter events, 0.1 us)
Async XLA Ops:
  0.0 19.3 %copy-start = (bf16[2048,2,2,128]{3,2,1,0:T(2,128)(2,1)S(1)}, bf16[2048,2,2,128]{3,2,1,0:T(2,128)(2,1)}, u32[]{:S(2)}) copy-start(bf16[2048,2,2,128]{3,2,1,0:T(2,128)(2,1)} %param.22) | copy-start | bytes 6291460
  0.0 14.7 %copy-start.7 = (f32[2048]{0:T(1024)S(1)}, f32[2048]{0:T(1024)}, u32[]{:S(2)}) copy-start(f32[2048]{0:T(1024)} %param.20) | copy-start | bytes 24580
  13.3 3.8 %copy-start.13 = (bf16[2048,1,2,128]{3,2,1,0:T(2,128)(2,1)S(1)}, bf16[2048,1,2,128]{3,2,1,0:T(2,128)(2,1)}, u32[]{:S(2)}) copy-start(bf16[2048,1,2,128]{3,2,1,0:T(2,128)(2,1)} %param.21) | copy-start | bytes 3145732
  14.8 2.7 %copy-start.8 = (bf16[2048,2,2]{0,2,1:T(2,128)(2,1)S(1)}, bf16[2048,2,2]{0,2,1:T(2,128)(2,1)}, u32[]{:S(2)}) copy-start(bf16[2048,2,2]{0,2,1:T(2,128)(2,1)} %param.23) | copy-start | bytes 49156
  16.2 0.9 copy-start.5
  17.1 2.0 %copy-start.3 = (bf16[3,8,8,2048]{3,2,1,0:T(8,128)(2,1)S(1)}, bf16[3,8,8,2048]{3,2,1,0:T(8,128)(2,1)}, u32[]{:S(2)}) copy-start(bf16[3,8,8,2048]{3,2,1,0:T(8,128)(2,1)} %gather_input.1) | copy-start | bytes 2359300
  19.3 0.7 copy-start.11
  19.3 0.7 copy-start.12
  19.3 0.7 copy-start.2
  20.0 3.4 %copy-start.1 = (f32[64,2,128,128]{3,2,1,0:T(8,128)S(1)}, f32[64,2,128,128]{3,2,1,0:T(8,128)}, u32[]{:S(2)}) copy-start(f32[64,2,128,128]{3,2,1,0:T(8,128)} %st_ref.1) | copy-start | bytes 25165828
  23.4 3.8 %copy-start.4 = (bf16[2,128,2048]{2,1,0:T(8,128)(2,1)S(1)}, bf16[2,128,2048]{2,1,0:T(8,128)(2,1)}, u32[]{:S(2)}) copy-start(bf16[2,128,2048]{2,1,0:T(8,128)(2,1)} %param.27) | copy-start | bytes 3145732
  27.2 1.3 copy-start.9
  27.2 2.0 %copy-start.10 = (f32[8,3,10]{2,0,1:T(8,128)S(1)}, f32[8,3,10]{2,0,1:T(8,128)}, u32[]{:S(2)}) copy-start(f32[8,3,10]{2,0,1:T(8,128)} %param.35) | copy-start | bytes 2884
  27.2 2.6 %copy-start.14 = (bf16[256]{0:T(256)(128)(2,1)S(1)}, bf16[256]{0:T(256)(128)(2,1)}, u32[]{:S(2)}) copy-start(bf16[256]{0:T(256)(128)(2,1)} %param.30) | copy-start | bytes 1540
  28.5 1.9 %copy-start.6 = (s32[4,32,16]{2,1,0:T(8,128)}, s32[4,32,16]{2,1,0:T(8,128)S(1)}, u32[]{:S(2)}) copy-start(s32[4,32,16]{2,1,0:T(8,128)S(1)} %tile.8) | copy-start | bytes 24580
